TPU v7x, 32 devices: a whole 2x2x4 slice. The times are simulated.
32 devices in a mesh: tm: 8 (over z, core), space: 4 (over y, x).
Axes of the slice: x: 2, y: 2, z: 4, core: 2. Of those that a mesh axis runs over, the one named last changes fastest.
Arguments:
- slab_starts: float32 [8, 4, 4, 4, 32, 128], P('tm', None, None, None, 'space'), may hold values from -1.4 to 6, as said below
- coarse_factor: float32 [4, 32, 128], P(None, 'space'), may hold values from 0.2 to 1
- blend_weight: float32 [32, 128], P('space'), may hold values from 0.2 to 0.9
- blend_flags: int32 [32, 128], P('space'), may hold values 0 or 1
Outputs:
- slab_ends: float32 [8, 4, 4, 4, 32, 128], P('tm', None, None, None, 'space')
- jump_norm: float32 [8], P('tm')
Inputs may be any that keep to these rules, and one draw needn't show every extreme that they name: `slab_starts`: at every node the density and the pressure lie between 0.5 and 2 and each velocity component between -0.7 and 0.7.
All inputs are finite; a program needn't handle non-finite values. No bound on the sum of `blend_flags` on one device may be relied on, other than what follows from the above.
Results may differ from a plain program's by a relative error of at most 0.0003.
Values sent between devices are 32-bit elements; how exact they have to be, the bound alone decides.
A program may use at most 128 MiB of HBM per device.

v0:
```python
import functools
import math

import jax
import jax.numpy as jnp
import numpy as np
from jax import lax
from jax.experimental import pallas as pl
from jax.experimental.pallas import tpu as pltpu
from jax.sharding import PartitionSpec as P

FSTEPS = 4
NODES = 4
VARS = 4

gamma_ratio = 1.4
step_size = 0.003
MESH = pl.DeviceIdType.MESH


def tables():
    inner = 1.0 / math.sqrt(5.0)
    points = np.array([-1.0, -inner, inner, 1.0])
    weights = np.array([1.0 / 6.0, 5.0 / 6.0, 5.0 / 6.0, 1.0 / 6.0])
    scales = [
        1.0 / np.prod([points[c] - points[k] for k in range(4) if k != c]) for c in range(4)
    ]
    derivative = np.zeros((4, 4))
    for r in range(4):
        for c in range(4):
            if r != c:
                derivative[r, c] = scales[c] / scales[r] / (points[r] - points[c])
    return derivative, weights


DERIVATIVE, WEIGHTS = tables()
QUAD = [[float(WEIGHTS[i] * WEIGHTS[j] / 4.0) for j in range(4)] for i in range(4)]


def rough(x):
    return pl.reciprocal(x, approx=True)


def inverse(x):
    r = pl.reciprocal(x, approx=True)
    return r * (2.0 - x * r)


def near_terms(a, b):
    total = a + b
    differ = b - a
    ratio = differ * rough(total)
    ratio = ratio * ratio
    series = 2.0 + ratio * (35.0 / 52.5 + ratio * (21.0 / 52.5 + ratio * (15.0 / 52.5)))
    return ratio < 0.0001, total, differ, series


def node_fields(u):
    rho, mx, my, energy = u
    ir = inverse(rho)
    vx = mx * ir
    vy = my * ir
    p = 0.4 * energy - 0.2 * (mx * vx + my * vy)
    beta = rho * inverse(p)
    warm = gamma_ratio * p * ir
    sound = warm * lax.rsqrt(warm)
    return (vx, vy, p, beta, jnp.log(rho), 2.5 * jnp.log(beta), sound)


def two_point(left, right, axis, scale):
    (ul, fl), (ur, fr) = left, right
    vnl, vtl = (fl[0], fl[1]) if axis == 0 else (fl[1], fl[0])
    vnr, vtr = (fr[0], fr[1]) if axis == 0 else (fr[1], fr[0])
    near, total, differ, series = near_terms(ul[0], ur[0])
    mean = jnp.where(near, total, differ) * inverse(jnp.where(near, series, fr[4] - fl[4]))
    near, total, differ, series = near_terms(fl[3], fr[3])
    thermal = jnp.where(near, 2.5 * series, fr[5] - fl[5]) * inverse(
        jnp.where(near, total, differ)
    )
    half_n = 0.5 * (vnl + vnr)
    half_t = 0.5 * (vtl + vtr)
    mass = mean * half_n
    if scale != 1.0:
        mass = mass * scale
    normal = mass * half_n + (0.5 * scale) * (fl[2] + fr[2])
    along = mass * half_t
    energy = mass * (0.5 * (vnl * vnr + vtl * vtr) + thermal) + (0.5 * scale) * (
        fl[2] * vnr + fr[2] * vnl
    )
    return (mass, normal, along, energy) if axis == 0 else (mass, along, normal, energy)


def face_flux(left, right, axis):
    (ul, fl), (ur, fr) = left, right
    centre = two_point(left, right, axis, 1.0)
    speed = 0.5 * jnp.maximum(jnp.abs(fl[axis]) + fl[6], jnp.abs(fr[axis]) + fr[6])
    return [centre[v] - speed * (ur[v] - ul[v]) for v in range(VARS)]


def physical(node, axis):
    u, f = node
    vn = f[axis]
    flux = [u[0] * vn, u[1] * vn, u[2] * vn, (u[3] + f[2]) * vn]
    flux[0] = u[1 + axis]
    flux[1 + axis] = flux[1 + axis] + f[2]
    return flux


def line_fluxes(nodes, axis, blend):
    pair = {}
    for a in range(4):
        for b in range(a + 1, 4):
            weight = float(2.0 * WEIGHTS[a] * DERIVATIVE[a, b])
            pair[a, b] = two_point(nodes[a], nodes[b], axis, weight)
    phys = [physical(node, axis) for node in nodes]
    fast = [jnp.abs(node[1][axis]) + node[1][6] for node in nodes]
    speeds = [jnp.maximum(fast[k], fast[k + 1]) for k in range(3)]
    result = [[], [], []]
    for v in range(VARS):
        far = pair[0, 3][v]
        head = pair[0, 2][v] + far
        tail = pair[1, 3][v]
        high = [pair[0, 1][v] + head, head + (pair[1, 2][v] + tail), (far + tail) + pair[2, 3][v]]
        for k in range(3):
            low = 0.5 * (
                (phys[k][v] + phys[k + 1][v])
                - speeds[k] * (nodes[k + 1][0][v] - nodes[k][0][v])
            )
            result[k].append(high[k] + blend * (low - high[k]))
    return result


def rolled(node, shift, axis):
    return tuple(tuple(pltpu.roll(x, shift, axis) for x in part) for part in node)


def coarse(u, factor):
    mean = None
    for i in range(4):
        for j in range(4):
            term = QUAD[i][j] * u[i][j]
            mean = term if mean is None else mean + term
    return [[mean + factor * (u[i][j] - mean) for j in range(4)] for i in range(4)]


def kernel(
    n_space,
    n_tm,
    o_ref,
    fac_ref,
    bw_ref,
    bf_ref,
    end_ref,
    norm_ref,
    st,
    fld,
    acc,
    blend_ref,
    low_ref,
    high_ref,
    from_left,
    from_right,
    edge_ref,
    corr,
    mate,
    pairs,
    start_ref,
    jump_ref,
    halo_send,
    halo_recv,
    corr_send,
    corr_recv,
    chain_send,
    chain_recv,
    fwd_send,
    fwd_recv,
    jump_send,
    jump_recv,
):
    rows, lanes = bw_ref.shape
    sp = lax.axis_index("space")
    tm = lax.axis_index("tm")
    core = lax.rem(tm, 2)
    z = lax.div(tm, 2)
    partner = tm + 1 - 2 * core
    chips = n_tm // 2
    left = lax.rem(sp + n_space - 1, n_space)
    right = lax.rem(sp + 1, n_space)
    takes = jnp.logical_and(core == 1, z > 0)
    gives = jnp.logical_and(core == 1, z < chips - 1)

    barrier = pltpu.get_barrier_semaphore()
    for k in range(1, n_space):
        other = lax.rem(sp + k, n_space)
        pl.semaphore_signal(barrier, inc=1, device_id={"space": other}, device_id_type=MESH)
    pl.semaphore_signal(barrier, inc=1, device_id={"tm": partner}, device_id_type=MESH)

    @pl.when(takes)
    def _():
        pl.semaphore_signal(barrier, inc=1, device_id={"tm": tm - 2}, device_id_type=MESH)

    @pl.when(gives)
    def _():
        pl.semaphore_signal(barrier, inc=1, device_id={"tm": tm + 2}, device_id_type=MESH)

    blend_ref[...] = bf_ref[...].astype(jnp.float32) * bw_ref[...]
    for v in range(VARS):
        for j in range(4):
            low = o_ref[0, v, 0, j, 0:1, :]
            high = o_ref[0, v, 3, j, rows - 1 : rows, :]
            for base in (0, 4):
                low_ref[0, v, base + j : base + j + 1, :] = low
                high_ref[0, v, base + j : base + j + 1, :] = high
    st[0] = o_ref[0]

    peers = n_space + takes.astype(jnp.int32) + gives.astype(jnp.int32)
    pl.semaphore_wait(barrier, peers)

    def halo(slot):
        return (
            pltpu.make_async_remote_copy(
                src_ref=low_ref.at[slot],
                dst_ref=from_right.at[slot],
                send_sem=halo_send.at[slot, 0],
                recv_sem=halo_recv.at[slot, 0],
                device_id={"space": left},
                device_id_type=MESH,
            ),
            pltpu.make_async_remote_copy(
                src_ref=high_ref.at[slot],
                dst_ref=from_left.at[slot],
                send_sem=halo_send.at[slot, 1],
                recv_sem=halo_recv.at[slot, 1],
                device_id={"space": right},
                device_id_type=MESH,
            ),
        )

    for copy in halo(0):
        copy.start()

    row_at = lax.broadcasted_iota(jnp.int32, (rows, lanes), 0)
    first_row = row_at == 0
    last_row = row_at == rows - 1
    upper_half = lax.broadcasted_iota(jnp.int32, (8, lanes), 0) < 4
    gain = [float(-2.0 / WEIGHTS[i]) for i in range(4)]

    def stage(s, _):
        now = lax.rem(s, 2)
        later = 1 - now
        keep = 0.5 * now.astype(jnp.float32)
        fresh = 1.0 - keep
        fresh_step = fresh * step_size

        def load(i, j):
            u = tuple(st[now, v, i, j] for v in range(VARS))
            return (u, tuple(fld[k, i, j] for k in range(7)))

        def fill(t, _):
            for j in range(4):
                values = node_fields(tuple(st[now, v, t, j] for v in range(VARS)))
                for k in range(7):
                    fld[k, t, j] = values[k]
            return 0

        lax.fori_loop(0, 4, fill, 0)

        def across(t, _):
            nodes = [load(i, t) for i in range(4)]
            inner = line_fluxes(nodes, 0, blend_ref[...])
            face = face_flux(rolled(nodes[3], 1, 0), nodes[0], 0)
            for v in range(VARS):
                lower = jnp.where(first_row, 0.0, face[v])
                upper = jnp.where(last_row, 0.0, pltpu.roll(face[v], rows - 1, 0))
                walls = [lower, inner[0][v], inner[1][v], inner[2][v], upper]
                for i in range(4):
                    acc[v, i, t] = gain[i] * (walls[i + 1] - walls[i])
            return 0

        lax.fori_loop(0, 4, across, 0)

        def upward(t, _):
            nodes = [load(t, j) for j in range(4)]
            inner = line_fluxes(nodes, 1, blend_ref[...])
            face = face_flux(rolled(nodes[3], 1, 1), nodes[0], 1)
            for v in range(VARS):
                upper = pltpu.roll(face[v], lanes - 1, 1)
                walls = [face[v], inner[0][v], inner[1][v], inner[2][v], upper]
                for j in range(4):
                    total = acc[v, t, j] + gain[j] * (walls[j + 1] - walls[j])
                    st[later, v, t, j] = (
                        keep * st[0, v, t, j] + fresh * nodes[j][0][v] + fresh_step * total
                    )
            return 0

        lax.fori_loop(0, 4, upward, 0)

        copies = halo(now)
        for copy in copies:
            copy.wait()

        uleft = tuple(
            jnp.where(upper_half, from_left[now, v], high_ref[now, v]) for v in range(VARS)
        )
        uright = tuple(
            jnp.where(upper_half, low_ref[now, v], from_right[now, v]) for v in range(VARS)
        )
        edge = face_flux((uleft, node_fields(uleft)), (uright, node_fields(uright)), 0)
        factor = jnp.where(upper_half, -gain[0] * fresh_step, gain[3] * fresh_step)
        for v in range(VARS):
            edge_ref[v] = factor * edge[v]
        for v in range(VARS):
            for j in range(4):
                low = st[later, v, 0, j, 0:1, :] + edge_ref[v, j : j + 1, :]
                high = st[later, v, 3, j, rows - 1 : rows, :] + edge_ref[v, 4 + j : 5 + j, :]
                st[later, v, 0, j, 0:1, :] = low
                st[later, v, 3, j, rows - 1 : rows, :] = high
                for base in (0, 4):
                    low_ref[later, v, base + j : base + j + 1, :] = low
                    high_ref[later, v, base + j : base + j + 1, :] = high

        @pl.when(s < 2 * FSTEPS - 1)
        def _():
            for copy in halo(later):
                copy.start()

        return 0

    lax.fori_loop(0, 2 * FSTEPS, stage, 0)

    def grid_of(view):
        return [[view(i, j) for j in range(4)] for i in range(4)]

    def pass_on(src, dst, send, recv, v, device):
        return pltpu.make_async_remote_copy(
            src_ref=src.at[v],
            dst_ref=dst.at[v],
            send_sem=send.at[v],
            recv_sem=recv.at[v],
            device_id={"tm": device},
            device_id_type=MESH,
        )

    def to_mate(v):
        return pass_on(corr, mate, corr_send, corr_recv, v, partner)

    def to_next(v):
        return pass_on(end_ref.at[0], start_ref, chain_send, chain_recv, v, tm + 2)

    def to_first(v):
        return pass_on(start_ref, start_ref, fwd_send, fwd_recv, v, partner)

    counted = jnp.where(tm == 0, 0.0, 1.0)
    for v in range(VARS):
        base = coarse(grid_of(lambda i, j: o_ref[0, v, i, j]), fac_ref[v])
        for i in range(4):
            for j in range(4):
                corr[v, i, j] = st[0, v, i, j] - counted * base[i][j]

        @pl.when(core == 0)
        def _():
            to_mate(v).start()

    jump_ref[0] = jnp.zeros((rows, lanes), jnp.float32)

    @pl.when(core == 0)
    def _():
        @pl.when(z == 0)
        def _():
            end_ref[0] = corr[...]

        @pl.when(z > 0)
        def _():
            total = jnp.zeros((rows, lanes), jnp.float32)
            for v in range(VARS):
                to_first(v).wait_recv()
                begun = grid_of(lambda i, j: start_ref[v, i, j])
                ended = coarse(begun, fac_ref[v])
                for i in range(4):
                    for j in range(4):
                        jump = begun[i][j] - o_ref[0, v, i, j]
                        total = total + QUAD[i][j] * (jump * jump)
                        end_ref[0, v, i, j] = ended[i][j] + corr[v, i, j]
            jump_ref[0] = total

        for v in range(VARS):
            to_mate(v).wait_send()

    @pl.when(core == 1)
    def _():
        @pl.when(z == 0)
        def _():
            start_ref[...] = jnp.zeros_like(start_ref)

        for v in range(VARS):
            to_mate(v).wait_recv()
            half = coarse(grid_of(lambda i, j: mate[v, i, j]), fac_ref[v])
            for i in range(4):
                for j in range(4):
                    pairs[v, i, j] = half[i][j] + corr[v, i, j]

        for v in range(VARS):

            @pl.when(z > 0)
            def _():
                to_next(v).wait_recv()
                to_first(v).start()

            factor = fac_ref[v]
            ended = coarse(grid_of(lambda i, j: start_ref[v, i, j]), factor * factor)
            for i in range(4):
                for j in range(4):
                    end_ref[0, v, i, j] = ended[i][j] + pairs[v, i, j]

            @pl.when(gives)
            def _():
                to_next(v).start()

        total = jnp.zeros((rows, lanes), jnp.float32)
        for v in range(VARS):
            begun = coarse(grid_of(lambda i, j: start_ref[v, i, j]), fac_ref[v])
            for i in range(4):
                for j in range(4):
                    jump = (begun[i][j] + mate[v, i, j]) - o_ref[0, v, i, j]
                    total = total + QUAD[i][j] * (jump * jump)
        jump_ref[0] = total

    def share(k):
        return pltpu.make_async_remote_copy(
            src_ref=jump_ref.at[0],
            dst_ref=jump_ref.at[k],
            send_sem=jump_send.at[k],
            recv_sem=jump_recv.at[k],
            device_id={"space": lax.rem(sp + k, n_space)},
            device_id_type=MESH,
        )

    for k in range(1, n_space):
        share(k).start()

    @pl.when(takes)
    def _():
        for v in range(VARS):
            to_first(v).wait_send()

    @pl.when(gives)
    def _():
        for v in range(VARS):
            to_next(v).wait_send()

    for k in range(1, n_space):
        share(k).wait()
    total = jump_ref[0]
    for k in range(1, n_space):
        total = total + jump_ref[k]
    total = jnp.sum(jnp.sum(total, axis=0, keepdims=True), axis=1, keepdims=True)
    norm_ref[...] = jnp.broadcast_to(
        jnp.sqrt(total * (1.0 / (n_space * rows * lanes))), norm_ref.shape
    )


def solution(mesh):
    n_tm = mesh.shape["tm"]
    n_space = mesh.shape["space"]

    def on_device(slab_starts, coarse_factor, blend_weight, blend_flags):
        rows, lanes = blend_weight.shape
        state = (VARS, NODES, NODES, rows, lanes)
        f32 = jnp.float32
        dma = pltpu.SemaphoreType.DMA
        vmem = pl.BlockSpec(memory_space=pltpu.VMEM)
        edges = pltpu.VMEM((2, VARS, 8, lanes), f32)
        ends, norm = pl.pallas_call(
            functools.partial(kernel, n_space, n_tm),
            out_shape=(
                jax.ShapeDtypeStruct((1,) + state, f32),
                jax.ShapeDtypeStruct((1, 128), f32),
            ),
            in_specs=[vmem] * 4,
            out_specs=(vmem, vmem),
            scratch_shapes=[
                pltpu.VMEM((2,) + state, f32),
                pltpu.VMEM((7, NODES, NODES, rows, lanes), f32),
                pltpu.VMEM(state, f32),
                pltpu.VMEM((rows, lanes), f32),
                edges,
                edges,
                edges,
                edges,
                pltpu.VMEM((VARS, 8, lanes), f32),
                pltpu.VMEM(state, f32),
                pltpu.VMEM(state, f32),
                pltpu.VMEM(state, f32),
                pltpu.VMEM(state, f32),
                pltpu.VMEM((n_space, rows, lanes), f32),
                dma((2, 2)),
                dma((2, 2)),
                dma((VARS,)),
                dma((VARS,)),
                dma((VARS,)),
                dma((VARS,)),
                dma((VARS,)),
                dma((VARS,)),
                dma((n_space,)),
                dma((n_space,)),
            ],
            compiler_params=pltpu.CompilerParams(
                collective_id=0, has_side_effects=True, vmem_limit_bytes=32 * 1024 * 1024
            ),
        )(slab_starts, coarse_factor, blend_weight, blend_flags)
        return ends, norm[0, :1]

    in_specs = (
        P("tm", None, None, None, "space", None),
        P(None, "space", None),
        P("space", None),
        P("space", None),
    )
    out_specs = (P("tm", None, None, None, "space", None), P("tm"))
    return jax.shard_map(
        on_device, mesh=mesh, in_specs=in_specs, out_specs=out_specs, check_vma=False
    )
```

profile of v0, /device:TPU:24, one launch (start us, length us, event | category | flops | bytes accessed | tf_op | source)
XLA Modules:
  0.0 47.7 jit_solution(2219739075163706837)
XLA Ops:
  0.6 0.0 copy-start
  0.6 0.9 %copy-done = f32[1,4,4,4,8,128]{5,4,3,2,1,0:T(8,128)S(1)} copy-done((f32[1,4,4,4,8,128]{5,4,3,2,1,0:T(8,128)S(1)}, f32[1,4,4,4,8,128]{5,4,3,2,1,0:T(8,128)}, u32[]{:S(2)}) %copy-start) | copy-done | bytes 262168
  1.6 0.0 copy-start.1
  1.6 0.7 %copy-done.1 = f32[4,8,128]{2,1,0:T(8,128)S(1)} copy-done((f32[4,8,128]{2,1,0:T(8,128)S(1)}, f32[4,8,128]{2,1,0:T(8,128)}, u32[]{:S(2)}) %copy-start.1) | copy-done | bytes 16408
  2.3 0.0 copy-start.2
  2.3 0.7 %copy-done.2 = f32[8,128]{1,0:T(8,128)S(1)} copy-done((f32[8,128]{1,0:T(8,128)S(1)}, f32[8,128]{1,0:T(8,128)}, u32[]{:S(2)}) %copy-start.2) | copy-done | bytes 4120
  3.0 0.0 copy-start.3
  3.0 0.7 %copy-done.3 = s32[8,128]{1,0:T(8,128)S(1)} copy-done((s32[8,128]{1,0:T(8,128)S(1)}, s32[8,128]{1,0:T(8,128)}, u32[]{:S(2)}) %copy-start.3) | copy-done | bytes 4120
  3.7 42.1 %shard_map.59 = (f32[1,4,4,4,8,128]{5,4,3,2,1,0:T(8,128)S(1)}, f32[1,128]{1,0:T(1,128)S(1)}) custom-call(f32[1,4,4,4,8,128]{5,4,3,2,1,0:T(8,128)S(1)} %copy-done, f32[4,8,128]{2,1,0:T(8,128)S(1)} %copy-done.1, f32[8,128]{1,0:T(8,128)S(1)} %copy-done.2, s32[8,128]{1,0:T(8,128)S(1)} %copy-done.3), custom_call_target="tpu_custom_call" | custom-call | tf_op jit(solution)/shard_map/pallas_call | solution.py:473
  45.8 0.7 %copy.8 = f32[1,4,4,4,8,128]{5,4,3,2,1,0:T(8,128)} copy(f32[1,4,4,4,8,128]{5,4,3,2,1,0:T(8,128)S(1)} %get-tuple-element.8) | data formatting | bytes 524288
Async XLA Ops:
  0.6 1.0 %copy-start = (f32[1,4,4,4,8,128]{5,4,3,2,1,0:T(8,128)S(1)}, f32[1,4,4,4,8,128]{5,4,3,2,1,0:T(8,128)}, u32[]{:S(2)}) copy-start(f32[1,4,4,4,8,128]{5,4,3,2,1,0:T(8,128)} %o_ref.1) | copy-start | bytes 786436
  1.6 0.7 %copy-start.1 = (f32[4,8,128]{2,1,0:T(8,128)S(1)}, f32[4,8,128]{2,1,0:T(8,128)}, u32[]{:S(2)}) copy-start(f32[4,8,128]{2,1,0:T(8,128)} %fac_ref.1) | copy-start | bytes 49156
  2.3 0.7 %copy-start.2 = (f32[8,128]{1,0:T(8,128)S(1)}, f32[8,128]{1,0:T(8,128)}, u32[]{:S(2)}) copy-start(f32[8,128]{1,0:T(8,128)} %bw_ref.1) | copy-start | bytes 12292
  3.0 0.7 %copy-start.3 = (s32[8,128]{1,0:T(8,128)S(1)}, s32[8,128]{1,0:T(8,128)}, u32[]{:S(2)}) copy-start(s32[8,128]{1,0:T(8,128)} %bf_ref.1) | copy-start | bytes 12292
where the time goes:
time: 48 us; the launch traced here: 47.7 us
  Pallas kernels  42.1 us (88%)
  local copies, waits for them, and re-layouts  3.74 us (8%)
  between operations  1.82 us (4%)
    pallas_call x1, Pallas kernels, on_device(): pl.pallas_call(functools.partial(kernel, n_space, n_tm), out_shape=(jax.S...  42.1 us
    unnamed x9, local copies, waits for them, and re-layouts  3.74 us

commit v1 on v0

--- a/solution.py
+++ b/solution.py
@@ -146,13 +146,18 @@
 def kernel(
     n_space,
     n_tm,
+    o_hbm,
+    fac_hbm,
+    bw_hbm,
+    bf_hbm,
+    end_ref,
+    norm_ref,
     o_ref,
     fac_ref,
     bw_ref,
     bf_ref,
-    end_ref,
-    norm_ref,
-    st,
+    u_ref,
+    w_ref,
     fld,
     acc,
     blend_ref,
@@ -176,8 +181,17 @@
     fwd_recv,
     jump_send,
     jump_recv,
+    load_sem,
 ):
     rows, lanes = bw_ref.shape
+    loads = [
+        pltpu.make_async_copy(src, dst, load_sem.at[k])
+        for k, (src, dst) in enumerate(
+            ((o_hbm, o_ref), (fac_hbm, fac_ref), (bw_hbm, bw_ref), (bf_hbm, bf_ref))
+        )
+    ]
+    for copy in loads:
+        copy.start()
     sp = lax.axis_index("space")
     tm = lax.axis_index("tm")
     core = lax.rem(tm, 2)
@@ -203,6 +217,8 @@
     def _():
         pl.semaphore_signal(barrier, inc=1, device_id={"tm": tm + 2}, device_id_type=MESH)
 
+    for copy in loads:
+        copy.wait()
     blend_ref[...] = bf_ref[...].astype(jnp.float32) * bw_ref[...]
     for v in range(VARS):
         for j in range(4):
@@ -211,7 +227,7 @@
             for base in (0, 4):
                 low_ref[0, v, base + j : base + j + 1, :] = low
                 high_ref[0, v, base + j : base + j + 1, :] = high
-    st[0] = o_ref[0]
+    u_ref[...] = o_ref[0]
 
     peers = n_space + takes.astype(jnp.int32) + gives.astype(jnp.int32)
     pl.semaphore_wait(barrier, peers)
@@ -245,29 +261,24 @@
     upper_half = lax.broadcasted_iota(jnp.int32, (8, lanes), 0) < 4
     gain = [float(-2.0 / WEIGHTS[i]) for i in range(4)]
 
-    def stage(s, _):
-        now = lax.rem(s, 2)
-        later = 1 - now
-        keep = 0.5 * now.astype(jnp.float32)
+    def stage(slot, src, dst, keep, more):
         fresh = 1.0 - keep
         fresh_step = fresh * step_size
 
         def load(i, j):
-            u = tuple(st[now, v, i, j] for v in range(VARS))
+            u = tuple(src[v, i, j] for v in range(VARS))
             return (u, tuple(fld[k, i, j] for k in range(7)))
 
-        def fill(t, _):
+        for i in range(4):
             for j in range(4):
-                values = node_fields(tuple(st[now, v, t, j] for v in range(VARS)))
+                values = node_fields(tuple(src[v, i, j] for v in range(VARS)))
                 for k in range(7):
-                    fld[k, t, j] = values[k]
-            return 0
-
-        lax.fori_loop(0, 4, fill, 0)
-
-        def across(t, _):
+                    fld[k, i, j] = values[k]
+        blend = blend_ref[...]
+
+        def across(t):
             nodes = [load(i, t) for i in range(4)]
-            inner = line_fluxes(nodes, 0, blend_ref[...])
+            inner = line_fluxes(nodes, 0, blend)
             face = face_flux(rolled(nodes[3], 1, 0), nodes[0], 0)
             for v in range(VARS):
                 lower = jnp.where(first_row, 0.0, face[v])
@@ -275,58 +286,63 @@
                 walls = [lower, inner[0][v], inner[1][v], inner[2][v], upper]
                 for i in range(4):
                     acc[v, i, t] = gain[i] * (walls[i + 1] - walls[i])
-            return 0
-
-        lax.fori_loop(0, 4, across, 0)
-
-        def upward(t, _):
+
+        def upward(t):
             nodes = [load(t, j) for j in range(4)]
-            inner = line_fluxes(nodes, 1, blend_ref[...])
+            inner = line_fluxes(nodes, 1, blend)
             face = face_flux(rolled(nodes[3], 1, 1), nodes[0], 1)
             for v in range(VARS):
                 upper = pltpu.roll(face[v], lanes - 1, 1)
                 walls = [face[v], inner[0][v], inner[1][v], inner[2][v], upper]
                 for j in range(4):
                     total = acc[v, t, j] + gain[j] * (walls[j + 1] - walls[j])
-                    st[later, v, t, j] = (
-                        keep * st[0, v, t, j] + fresh * nodes[j][0][v] + fresh_step * total
-                    )
-            return 0
-
-        lax.fori_loop(0, 4, upward, 0)
-
-        copies = halo(now)
-        for copy in copies:
+                    value = fresh * nodes[j][0][v] + fresh_step * total
+                    if keep:
+                        value = value + keep * dst[v, t, j]
+                    dst[v, t, j] = value
+
+        for t in range(4):
+            across(t)
+        for t in (1, 2):
+            upward(t)
+
+        for copy in halo(slot):
             copy.wait()
 
         uleft = tuple(
-            jnp.where(upper_half, from_left[now, v], high_ref[now, v]) for v in range(VARS)
+            jnp.where(upper_half, from_left[slot, v], high_ref[slot, v]) for v in range(VARS)
         )
         uright = tuple(
-            jnp.where(upper_half, low_ref[now, v], from_right[now, v]) for v in range(VARS)
+            jnp.where(upper_half, low_ref[slot, v], from_right[slot, v]) for v in range(VARS)
         )
         edge = face_flux((uleft, node_fields(uleft)), (uright, node_fields(uright)), 0)
         factor = jnp.where(upper_half, -gain[0] * fresh_step, gain[3] * fresh_step)
         for v in range(VARS):
             edge_ref[v] = factor * edge[v]
+        for t in (0, 3):
+            upward(t)
+        other = 1 - slot
         for v in range(VARS):
             for j in range(4):
-                low = st[later, v, 0, j, 0:1, :] + edge_ref[v, j : j + 1, :]
-                high = st[later, v, 3, j, rows - 1 : rows, :] + edge_ref[v, 4 + j : 5 + j, :]
-                st[later, v, 0, j, 0:1, :] = low
-                st[later, v, 3, j, rows - 1 : rows, :] = high
+                low = dst[v, 0, j, 0:1, :] + edge_ref[v, j : j + 1, :]
+                high = dst[v, 3, j, rows - 1 : rows, :] + edge_ref[v, 4 + j : 5 + j, :]
+                dst[v, 0, j, 0:1, :] = low
+                dst[v, 3, j, rows - 1 : rows, :] = high
                 for base in (0, 4):
-                    low_ref[later, v, base + j : base + j + 1, :] = low
-                    high_ref[later, v, base + j : base + j + 1, :] = high
-
-        @pl.when(s < 2 * FSTEPS - 1)
+                    low_ref[other, v, base + j : base + j + 1, :] = low
+                    high_ref[other, v, base + j : base + j + 1, :] = high
+
+        @pl.when(more)
         def _():
-            for copy in halo(later):
+            for copy in halo(other):
                 copy.start()
 
+    def fine_step(step, _):
+        stage(0, u_ref, w_ref, 0.0, step < FSTEPS)
+        stage(1, w_ref, u_ref, 0.5, step < FSTEPS - 1)
         return 0
 
-    lax.fori_loop(0, 2 * FSTEPS, stage, 0)
+    lax.fori_loop(0, FSTEPS, fine_step, 0)
 
     def grid_of(view):
         return [[view(i, j) for j in range(4)] for i in range(4)]
@@ -355,7 +371,7 @@
         base = coarse(grid_of(lambda i, j: o_ref[0, v, i, j]), fac_ref[v])
         for i in range(4):
             for j in range(4):
-                corr[v, i, j] = st[0, v, i, j] - counted * base[i][j]
+                corr[v, i, j] = u_ref[v, i, j] - counted * base[i][j]
 
         @pl.when(core == 0)
         def _():
@@ -476,10 +492,15 @@
                 jax.ShapeDtypeStruct((1,) + state, f32),
                 jax.ShapeDtypeStruct((1, 128), f32),
             ),
-            in_specs=[vmem] * 4,
+            in_specs=[pl.BlockSpec(memory_space=pltpu.HBM)] * 4,
             out_specs=(vmem, vmem),
             scratch_shapes=[
-                pltpu.VMEM((2,) + state, f32),
+                pltpu.VMEM((1,) + state, f32),
+                pltpu.VMEM(coarse_factor.shape, f32),
+                pltpu.VMEM(blend_weight.shape, f32),
+                pltpu.VMEM(blend_flags.shape, blend_flags.dtype),
+                pltpu.VMEM(state, f32),
+                pltpu.VMEM(state, f32),
                 pltpu.VMEM((7, NODES, NODES, rows, lanes), f32),
                 pltpu.VMEM(state, f32),
                 pltpu.VMEM((rows, lanes), f32),
@@ -503,6 +524,7 @@
                 dma((VARS,)),
                 dma((n_space,)),
                 dma((n_space,)),
+                dma((4,)),
             ],
             compiler_params=pltpu.CompilerParams(
                 collective_id=0, has_side_effects=True, vmem_limit_bytes=32 * 1024 * 1024

time: 48 us -> 49.7 us (1.035)
  Pallas kernels: 42.1 us -> 43.9 us
    pallas_call x1, Pallas kernels: 42.1 us -> 43.9 us  [on_device(): pl.pallas_call(functools.partial(kernel, n_space, n_tm), out_shape=(jax.S...]
where the time goes in v1:
time: 49.7 us; the launch traced here: 49.4 us
  Pallas kernels  43.9 us (88%)
  local copies, waits for them, and re-layouts  3.74 us (8%)
  between operations  1.82 us (4%)
    pallas_call x1, Pallas kernels, on_device(): pl.pallas_call(functools.partial(kernel, n_space, n_tm), out_shape=(jax.S...  43.9 us
    unnamed x9, local copies, waits for them, and re-layouts  3.74 us

profile of v1, /device:TPU:24, one launch (start us, length us, event | category | flops | bytes accessed | tf_op | source)
XLA Modules:
  0.0 49.4 jit_solution(14074314257856188309)
XLA Ops:
  0.6 0.0 copy-start
  0.6 0.9 %copy-done = f32[1,4,4,4,8,128]{5,4,3,2,1,0:T(8,128)S(1)} copy-done((f32[1,4,4,4,8,128]{5,4,3,2,1,0:T(8,128)S(1)}, f32[1,4,4,4,8,128]{5,4,3,2,1,0:T(8,128)}, u32[]{:S(2)}) %copy-start) | copy-done | bytes 262168
  1.6 0.0 copy-start.1
  1.6 0.7 %copy-done.1 = f32[4,8,128]{2,1,0:T(8,128)S(1)} copy-done((f32[4,8,128]{2,1,0:T(8,128)S(1)}, f32[4,8,128]{2,1,0:T(8,128)}, u32[]{:S(2)}) %copy-start.1) | copy-done | bytes 16408
  2.3 0.0 copy-start.2
  2.3 0.7 %copy-done.2 = f32[8,128]{1,0:T(8,128)S(1)} copy-done((f32[8,128]{1,0:T(8,128)S(1)}, f32[8,128]{1,0:T(8,128)}, u32[]{:S(2)}) %copy-start.2) | copy-done | bytes 4120
  3.0 0.0 copy-start.3
  3.0 0.7 %copy-done.3 = s32[8,128]{1,0:T(8,128)S(1)} copy-done((s32[8,128]{1,0:T(8,128)S(1)}, s32[8,128]{1,0:T(8,128)}, u32[]{:S(2)}) %copy-start.3) | copy-done | bytes 4120
  3.7 43.9 %shard_map.59 = (f32[1,4,4,4,8,128]{5,4,3,2,1,0:T(8,128)S(1)}, f32[1,128]{1,0:T(1,128)S(1)}) custom-call(f32[1,4,4,4,8,128]{5,4,3,2,1,0:T(8,128)S(1)} %copy-done, f32[4,8,128]{2,1,0:T(8,128)S(1)} %copy-done.1, f32[8,128]{1,0:T(8,128)S(1)} %copy-done.2, s32[8,128]{1,0:T(8,128)S(1)} %copy-done.3), custom_call_target="tpu_custom_call" | custom-call | tf_op jit(solution)/shard_map/pallas_call | solution.py:489
  47.6 0.7 %copy.8 = f32[1,4,4,4,8,128]{5,4,3,2,1,0:T(8,128)} copy(f32[1,4,4,4,8,128]{5,4,3,2,1,0:T(8,128)S(1)} %get-tuple-element.8) | data formatting | bytes 524288
Async XLA Ops:
  0.6 1.0 %copy-start = (f32[1,4,4,4,8,128]{5,4,3,2,1,0:T(8,128)S(1)}, f32[1,4,4,4,8,128]{5,4,3,2,1,0:T(8,128)}, u32[]{:S(2)}) copy-start(f32[1,4,4,4,8,128]{5,4,3,2,1,0:T(8,128)} %o_hbm.1) | copy-start | bytes 786436
  1.6 0.7 %copy-start.1 = (f32[4,8,128]{2,1,0:T(8,128)S(1)}, f32[4,8,128]{2,1,0:T(8,128)}, u32[]{:S(2)}) copy-start(f32[4,8,128]{2,1,0:T(8,128)} %fac_hbm.1) | copy-start | bytes 49156
  2.3 0.7 %copy-start.2 = (f32[8,128]{1,0:T(8,128)S(1)}, f32[8,128]{1,0:T(8,128)}, u32[]{:S(2)}) copy-start(f32[8,128]{1,0:T(8,128)} %bw_hbm.1) | copy-start | bytes 12292
  3.0 0.7 %copy-start.3 = (s32[8,128]{1,0:T(8,128)S(1)}, s32[8,128]{1,0:T(8,128)}, u32[]{:S(2)}) copy-start(s32[8,128]{1,0:T(8,128)} %bf_hbm.1) | copy-start | bytes 12292

commit v2 on v1

--- a/solution.py
+++ b/solution.py
@@ -166,6 +166,8 @@
     from_left,
     from_right,
     edge_ref,
+    own_ref,
+    near_ref,
     corr,
     mate,
     pairs,
@@ -220,14 +222,22 @@
     for copy in loads:
         copy.wait()
     blend_ref[...] = bf_ref[...].astype(jnp.float32) * bw_ref[...]
-    for v in range(VARS):
-        for j in range(4):
-            low = o_ref[0, v, 0, j, 0:1, :]
-            high = o_ref[0, v, 3, j, rows - 1 : rows, :]
-            for base in (0, 4):
-                low_ref[0, v, base + j : base + j + 1, :] = low
-                high_ref[0, v, base + j : base + j + 1, :] = high
+    for slot in range(2):
+        low_ref[slot, 2 * VARS] = jnp.broadcast_to(blend_ref[0:1, :], (8, lanes))
+        high_ref[slot, 2 * VARS] = jnp.broadcast_to(blend_ref[rows - 1 : rows, :], (8, lanes))
+
+    def pack(slot):
+        for v in range(VARS):
+            for d in range(4):
+                for j in range(4):
+                    at = 4 * (d % 2) + j
+                    low_ref[slot, 2 * v + d // 2, at : at + 1, :] = u_ref[v, d, j, 0:1, :]
+                    high_ref[slot, 2 * v + d // 2, at : at + 1, :] = u_ref[
+                        v, 3 - d, j, rows - 1 : rows, :
+                    ]
+
     u_ref[...] = o_ref[0]
+    pack(0)
 
     peers = n_space + takes.astype(jnp.int32) + gives.astype(jnp.int32)
     pl.semaphore_wait(barrier, peers)
@@ -261,7 +271,74 @@
     upper_half = lax.broadcasted_iota(jnp.int32, (8, lanes), 0) < 4
     gain = [float(-2.0 / WEIGHTS[i]) for i in range(4)]
 
-    def stage(slot, src, dst, keep, more):
+    sub = lax.rem(lax.broadcasted_iota(jnp.int32, (8, lanes), 0), 4)
+
+    def by_node(values):
+        return jnp.where(
+            sub == 0, values[0], jnp.where(sub == 1, values[1], jnp.where(sub == 2, values[2], values[3]))
+        )
+
+    def choose(mask, left, right):
+        return tuple(
+            tuple(jnp.where(mask, a, b) for a, b in zip(p, q)) for p, q in zip(left, right)
+        )
+
+    def lane_rolled(node, shift):
+        return rolled(node, shift, 1)
+
+    def coefficient(a, b):
+        return float(2.0 * WEIGHTS[a] * DERIVATIVE[a, b])
+
+    side = jnp.where(upper_half, 1.0, -1.0)
+
+    def outside(nodes, edge, blend):
+        near = nodes[0]
+        high = [0.0] * VARS
+        for d in (1, 2, 3):
+            term = two_point(nodes[d], near, 0, coefficient(3 - d, 3))
+            high = [high[v] + term[v] for v in range(VARS)]
+        phys = [physical(nodes[d], 0) for d in (0, 1)]
+        fast = [jnp.abs(nodes[d][1][0]) + nodes[d][1][6] for d in (0, 1)]
+        speed = side * jnp.maximum(fast[0], fast[1])
+        rate = []
+        for v in range(VARS):
+            low = 0.5 * (phys[0][v] + phys[1][v] - speed * (near[0][v] - nodes[1][0][v]))
+            inner = high[v] + blend * (low - high[v])
+            rate.append((gain[3] * side) * (edge[v] - inner))
+
+        wrapped = rolled(near, 5, 0)
+        before = choose(sub == 0, lane_rolled(wrapped, 1), rolled(near, 1, 0))
+        first = two_point(before, near, 1, 1.0)
+        second = two_point(choose(sub == 0, wrapped, rolled(near, 2, 0)), near, 1, 1.0)
+        first_scale = by_node([0.0, coefficient(0, 1), coefficient(1, 2), coefficient(2, 3)])
+        second_scale = by_node([coefficient(0, 3), 0.0, coefficient(0, 2), coefficient(1, 3)])
+        before_phys, near_phys = physical(before, 1), physical(near, 1)
+        speed = 0.5 * jnp.maximum(
+            jnp.abs(before[1][1]) + before[1][6], jnp.abs(near[1][1]) + near[1][6]
+        )
+        gains = by_node(gain)
+        result = []
+        for v in range(VARS):
+            damping = speed * (near[0][v] - before[0][v])
+            far = second_scale * second[v]
+            high = first_scale * first[v] + jnp.where(sub >= 2, far, 0.0)
+            high = high + jnp.where(
+                jnp.logical_or(sub == 1, sub == 2), pltpu.roll(far, 7, 0), 0.0
+            )
+            high = high + by_node(
+                [0.0, pltpu.roll(far, 1, 0), pltpu.roll(far, 2, 0), pltpu.roll(far, 3, 0)]
+            )
+            low = 0.5 * (before_phys[v] + near_phys[v]) - damping
+            wall = jnp.where(sub == 0, first[v] - damping, high + blend * (low - high))
+            above = jnp.where(
+                sub == 3,
+                pltpu.roll(pltpu.roll(wall, 3, 0), lanes - 1, 1),
+                pltpu.roll(wall, 7, 0),
+            )
+            result.append(near[0][v] + step_size * (rate[v] + gains * (above - wall)))
+        return result
+
+    def stage(first, slot, src, dst, keep):
         fresh = 1.0 - keep
         fresh_step = fresh * step_size
 
@@ -306,40 +383,66 @@
         for t in (1, 2):
             upward(t)
 
-        for copy in halo(slot):
-            copy.wait()
-
-        uleft = tuple(
-            jnp.where(upper_half, from_left[slot, v], high_ref[slot, v]) for v in range(VARS)
-        )
-        uright = tuple(
-            jnp.where(upper_half, low_ref[slot, v], from_right[slot, v]) for v in range(VARS)
-        )
-        edge = face_flux((uleft, node_fields(uleft)), (uright, node_fields(uright)), 0)
+        if first:
+            for copy in halo(slot):
+                copy.wait()
+
+            def packed(v, d):
+                left_tile = from_left[slot, 2 * v + d // 2]
+                right_tile = from_right[slot, 2 * v + d // 2]
+                if d % 2:
+                    left_tile = pltpu.roll(left_tile, 4, 0)
+                else:
+                    right_tile = pltpu.roll(right_tile, 4, 0)
+                return jnp.where(upper_half, left_tile, right_tile)
+
+            values = [tuple(packed(v, d) for v in range(VARS)) for d in range(4)]
+            beyond = [(u, node_fields(u)) for u in values]
+            own = tuple(
+                jnp.where(upper_half, low_ref[slot, 2 * v], pltpu.roll(high_ref[slot, 2 * v], 4, 0))
+                for v in range(VARS)
+            )
+        else:
+            u = tuple(near_ref[v] for v in range(VARS))
+            beyond = [(u, node_fields(u))]
+            own = tuple(own_ref[v] for v in range(VARS))
+        own = (own, node_fields(own))
+        edge = face_flux(
+            choose(upper_half, beyond[0], own), choose(upper_half, own, beyond[0]), 0
+        )
         factor = jnp.where(upper_half, -gain[0] * fresh_step, gain[3] * fresh_step)
         for v in range(VARS):
             edge_ref[v] = factor * edge[v]
+        if first:
+            outer_blend = jnp.where(
+                upper_half, from_left[slot, 2 * VARS], from_right[slot, 2 * VARS]
+            )
+            stepped = outside(beyond, edge, outer_blend)
+            for v in range(VARS):
+                near_ref[v] = stepped[v]
         for t in (0, 3):
             upward(t)
-        other = 1 - slot
         for v in range(VARS):
             for j in range(4):
                 low = dst[v, 0, j, 0:1, :] + edge_ref[v, j : j + 1, :]
                 high = dst[v, 3, j, rows - 1 : rows, :] + edge_ref[v, 4 + j : 5 + j, :]
                 dst[v, 0, j, 0:1, :] = low
                 dst[v, 3, j, rows - 1 : rows, :] = high
-                for base in (0, 4):
-                    low_ref[other, v, base + j : base + j + 1, :] = low
-                    high_ref[other, v, base + j : base + j + 1, :] = high
-
-        @pl.when(more)
+                if first:
+                    own_ref[v, j : j + 1, :] = low
+                    own_ref[v, 4 + j : 5 + j, :] = high
+
+    def fine_step(step, _):
+        slot = lax.rem(step, 2)
+        stage(True, slot, u_ref, w_ref, 0.0)
+        stage(False, slot, w_ref, u_ref, 0.5)
+
+        @pl.when(step < FSTEPS - 1)
         def _():
-            for copy in halo(other):
+            pack(1 - slot)
+            for copy in halo(1 - slot):
                 copy.start()
 
-    def fine_step(step, _):
-        stage(0, u_ref, w_ref, 0.0, step < FSTEPS)
-        stage(1, w_ref, u_ref, 0.5, step < FSTEPS - 1)
         return 0
 
     lax.fori_loop(0, FSTEPS, fine_step, 0)
@@ -485,7 +588,7 @@
         f32 = jnp.float32
         dma = pltpu.SemaphoreType.DMA
         vmem = pl.BlockSpec(memory_space=pltpu.VMEM)
-        edges = pltpu.VMEM((2, VARS, 8, lanes), f32)
+        edges = pltpu.VMEM((2, 2 * VARS + 1, 8, lanes), f32)
         ends, norm = pl.pallas_call(
             functools.partial(kernel, n_space, n_tm),
             out_shape=(
@@ -509,6 +612,8 @@
                 edges,
                 edges,
                 pltpu.VMEM((VARS, 8, lanes), f32),
+                pltpu.VMEM((VARS, 8, lanes), f32),
+                pltpu.VMEM((VARS, 8, lanes), f32),
                 pltpu.VMEM(state, f32),
                 pltpu.VMEM(state, f32),
                 pltpu.VMEM(state, f32),
@@ -527,7 +632,7 @@
                 dma((4,)),
             ],
             compiler_params=pltpu.CompilerParams(
-                collective_id=0, has_side_effects=True, vmem_limit_bytes=32 * 1024 * 1024
+                collective_id=0, has_side_effects=True, vmem_limit_bytes=64 * 1024 * 1024
             ),
         )(slab_starts, coarse_factor, blend_weight, blend_flags)
         return ends, norm[0, :1]

time: 49.7 us -> 39.6 us (0.80)
  Pallas kernels: 43.9 us -> 35.9 us
  local copies, waits for them, and re-layouts: 3.74 us -> 1.68 us
    pallas_call x1, Pallas kernels: 43.9 us -> 35.9 us  [on_device(): pl.pallas_call(functools.partial(kernel, n_space, n_tm), out_shape=(jax.S...]
    unnamed x9 -> x3, local copies, waits for them, and re-layouts: 3.74 us -> 1.68 us
where the time goes in v2:
time: 39.6 us; the launch traced here: 39.4 us
  Pallas kernels  35.9 us (91%)
  between operations  1.81 us (5%)
  local copies, waits for them, and re-layouts  1.68 us (4%)
    pallas_call x1, Pallas kernels, on_device(): pl.pallas_call(functools.partial(kernel, n_space, n_tm), out_shape=(jax.S...  35.9 us
    unnamed x3, local copies, waits for them, and re-layouts  1.68 us

profile of v2, /device:TPU:24, one launch (start us, length us, event | category | flops | bytes accessed | tf_op | source)
XLA Modules:
  0.0 39.4 jit_solution(7115871266784666312)
XLA Ops:
  0.6 35.9 %shard_map.59 = (f32[1,4,4,4,8,128]{5,4,3,2,1,0:T(8,128)}, f32[1,128]{1,0:T(1,128)}) custom-call(f32[1,4,4,4,8,128]{5,4,3,2,1,0:T(8,128)} %o_hbm.1, f32[4,8,128]{2,1,0:T(8,128)} %fac_hbm.1, f32[8,128]{1,0:T(8,128)} %bw_hbm.1, s32[8,128]{1,0:T(8,128)} %bf_hbm.1), custom_call_target="tpu_custom_call" | custom-call | tf_op jit(solution)/shard_map/pallas_call | solution.py:592
  36.6 0.0 copy-start
  36.6 1.7 %copy.8 = f32[1,4,4,4,8,128]{5,4,3,2,1,0:T(8,128)} copy(f32[1,4,4,4,8,128]{5,4,3,2,1,0:T(8,128)} %get-tuple-element.8) | data formatting | bytes 524288
  38.3 0.0 copy-done
Async XLA Ops:
  36.6 1.7 %copy-start = (f32[1,128]{1,0:T(1,128)S(1)}, f32[1,128]{1,0:T(1,128)}, u32[]{:S(2)}) copy-start(f32[1,128]{1,0:T(1,128)} %get-tuple-element.5) | copy-start | bytes 1540

commit v3 on v2

--- a/solution.py
+++ b/solution.py
@@ -150,8 +150,11 @@
     fac_hbm,
     bw_hbm,
     bf_hbm,
+    end_hbm,
+    norm_ref,
     end_ref,
-    norm_ref,
+    mean_in,
+    mean_out,
     o_ref,
     fac_ref,
     bw_ref,
@@ -184,6 +187,7 @@
     jump_send,
     jump_recv,
     load_sem,
+    store_sem,
 ):
     rows, lanes = bw_ref.shape
     loads = [
@@ -450,24 +454,47 @@
     def grid_of(view):
         return [[view(i, j) for j in range(4)] for i in range(4)]
 
-    def pass_on(src, dst, send, recv, v, device):
+    def pass_on(src, dst, send, recv, k, device):
         return pltpu.make_async_remote_copy(
-            src_ref=src.at[v],
-            dst_ref=dst.at[v],
-            send_sem=send.at[v],
-            recv_sem=recv.at[v],
+            src_ref=src,
+            dst_ref=dst,
+            send_sem=send.at[k],
+            recv_sem=recv.at[k],
             device_id={"tm": device},
             device_id_type=MESH,
         )
 
     def to_mate(v):
-        return pass_on(corr, mate, corr_send, corr_recv, v, partner)
-
-    def to_next(v):
-        return pass_on(end_ref.at[0], start_ref, chain_send, chain_recv, v, tm + 2)
-
-    def to_first(v):
-        return pass_on(start_ref, start_ref, fwd_send, fwd_recv, v, partner)
+        return pass_on(corr.at[v], mate.at[v], corr_send, corr_recv, v, partner)
+
+    def mean_to_next(v):
+        return pass_on(
+            mean_out.at[v], mean_in.at[v], chain_send, chain_recv, VARS * 4 + v, tm + 2
+        )
+
+    def to_next(v, i):
+        return pass_on(
+            end_ref.at[0, v, i], start_ref.at[v, i], chain_send, chain_recv, v * 4 + i, tm + 2
+        )
+
+    def to_first(v, i):
+        return pass_on(
+            start_ref.at[v, i], start_ref.at[v, i], fwd_send, fwd_recv, v * 4 + i, partner
+        )
+
+    def store(v):
+        return pltpu.make_async_copy(end_ref.at[0, v], end_hbm.at[0, v], store_sem.at[v])
+
+    def pair_up(v):
+        to_mate(v).wait_recv()
+        half = coarse(grid_of(lambda i, j: mate[v, i, j]), fac_ref[v])
+        values = [[half[i][j] + corr[v, i, j] for j in range(4)] for i in range(4)]
+        mean = None
+        for i in range(4):
+            for j in range(4):
+                term = QUAD[i][j] * values[i][j]
+                mean = term if mean is None else mean + term
+        return values, mean
 
     counted = jnp.where(tm == 0, 0.0, 1.0)
     for v in range(VARS):
@@ -487,12 +514,15 @@
         @pl.when(z == 0)
         def _():
             end_ref[0] = corr[...]
+            for v in range(VARS):
+                store(v).start()
 
         @pl.when(z > 0)
         def _():
             total = jnp.zeros((rows, lanes), jnp.float32)
             for v in range(VARS):
-                to_first(v).wait_recv()
+                for i in range(4):
+                    to_first(v, i).wait_recv()
                 begun = grid_of(lambda i, j: start_ref[v, i, j])
                 ended = coarse(begun, fac_ref[v])
                 for i in range(4):
@@ -500,49 +530,75 @@
                         jump = begun[i][j] - o_ref[0, v, i, j]
                         total = total + QUAD[i][j] * (jump * jump)
                         end_ref[0, v, i, j] = ended[i][j] + corr[v, i, j]
+                store(v).start()
             jump_ref[0] = total
-
-        for v in range(VARS):
-            to_mate(v).wait_send()
 
     @pl.when(core == 1)
     def _():
         @pl.when(z == 0)
         def _():
-            start_ref[...] = jnp.zeros_like(start_ref)
-
-        for v in range(VARS):
-            to_mate(v).wait_recv()
-            half = coarse(grid_of(lambda i, j: mate[v, i, j]), fac_ref[v])
-            for i in range(4):
-                for j in range(4):
-                    pairs[v, i, j] = half[i][j] + corr[v, i, j]
-
-        for v in range(VARS):
-
-            @pl.when(z > 0)
-            def _():
-                to_next(v).wait_recv()
-                to_first(v).start()
-
-            factor = fac_ref[v]
-            ended = coarse(grid_of(lambda i, j: start_ref[v, i, j]), factor * factor)
-            for i in range(4):
-                for j in range(4):
-                    end_ref[0, v, i, j] = ended[i][j] + pairs[v, i, j]
-
-            @pl.when(gives)
-            def _():
-                to_next(v).start()
-
-        total = jnp.zeros((rows, lanes), jnp.float32)
-        for v in range(VARS):
-            begun = coarse(grid_of(lambda i, j: start_ref[v, i, j]), fac_ref[v])
-            for i in range(4):
-                for j in range(4):
-                    jump = (begun[i][j] + mate[v, i, j]) - o_ref[0, v, i, j]
-                    total = total + QUAD[i][j] * (jump * jump)
-        jump_ref[0] = total
+            total = jnp.zeros((rows, lanes), jnp.float32)
+            for v in range(VARS):
+                values, mean = pair_up(v)
+                mean_out[v] = mean
+                for i in range(4):
+                    for j in range(4):
+                        end_ref[0, v, i, j] = values[i][j]
+
+                @pl.when(gives)
+                def _():
+                    mean_to_next(v).start()
+                    for i in range(4):
+                        to_next(v, i).start()
+
+                store(v).start()
+                for i in range(4):
+                    for j in range(4):
+                        jump = mate[v, i, j] - o_ref[0, v, i, j]
+                        total = total + QUAD[i][j] * (jump * jump)
+            jump_ref[0] = total
+
+        @pl.when(z > 0)
+        def _():
+            for v in range(VARS):
+                values, mean = pair_up(v)
+                mean_out[v] = mean
+                for i in range(4):
+                    for j in range(4):
+                        pairs[v, i, j] = values[i][j]
+
+            total = jnp.zeros((rows, lanes), jnp.float32)
+            for v in range(VARS):
+                mean_to_next(v).wait_recv()
+                mean = mean_in[v]
+                mean_out[v] = mean + mean_out[v]
+
+                @pl.when(gives)
+                def _():
+                    mean_to_next(v).start()
+
+                factor = fac_ref[v]
+                twice = factor * factor
+                for i in range(4):
+                    to_next(v, i).wait_recv()
+                    for j in range(4):
+                        end_ref[0, v, i, j] = (
+                            mean + twice * (start_ref[v, i, j] - mean) + pairs[v, i, j]
+                        )
+
+                    @pl.when(gives)
+                    def _():
+                        to_next(v, i).start()
+
+                    to_first(v, i).start()
+
+                store(v).start()
+                begun = coarse(grid_of(lambda i, j: start_ref[v, i, j]), factor)
+                for i in range(4):
+                    for j in range(4):
+                        jump = (begun[i][j] + mate[v, i, j]) - o_ref[0, v, i, j]
+                        total = total + QUAD[i][j] * (jump * jump)
+            jump_ref[0] = total
 
     def share(k):
         return pltpu.make_async_remote_copy(
@@ -557,15 +613,26 @@
     for k in range(1, n_space):
         share(k).start()
 
+    @pl.when(core == 0)
+    def _():
+        for v in range(VARS):
+            to_mate(v).wait_send()
+
     @pl.when(takes)
     def _():
         for v in range(VARS):
-            to_first(v).wait_send()
+            for i in range(4):
+                to_first(v, i).wait_send()
 
     @pl.when(gives)
     def _():
         for v in range(VARS):
-            to_next(v).wait_send()
+            mean_to_next(v).wait_send()
+            for i in range(4):
+                to_next(v, i).wait_send()
+
+    for v in range(VARS):
+        store(v).wait()
 
     for k in range(1, n_space):
         share(k).wait()
@@ -596,8 +663,11 @@
                 jax.ShapeDtypeStruct((1, 128), f32),
             ),
             in_specs=[pl.BlockSpec(memory_space=pltpu.HBM)] * 4,
-            out_specs=(vmem, vmem),
+            out_specs=(pl.BlockSpec(memory_space=pltpu.HBM), vmem),
             scratch_shapes=[
+                pltpu.VMEM((1,) + state, f32),
+                pltpu.VMEM((VARS, rows, lanes), f32),
+                pltpu.VMEM((VARS, rows, lanes), f32),
                 pltpu.VMEM((1,) + state, f32),
                 pltpu.VMEM(coarse_factor.shape, f32),
                 pltpu.VMEM(blend_weight.shape, f32),
@@ -623,13 +693,14 @@
                 dma((2, 2)),
                 dma((VARS,)),
                 dma((VARS,)),
-                dma((VARS,)),
-                dma((VARS,)),
-                dma((VARS,)),
-                dma((VARS,)),
+                dma((VARS * 5,)),
+                dma((VARS * 5,)),
+                dma((VARS * 4,)),
+                dma((VARS * 4,)),
                 dma((n_space,)),
                 dma((n_space,)),
                 dma((4,)),
+                dma((VARS,)),
             ],
             compiler_params=pltpu.CompilerParams(
                 collective_id=0, has_side_effects=True, vmem_limit_bytes=64 * 1024 * 1024

time: 39.6 us -> 38.7 us (0.977)
  Pallas kernels: 35.9 us -> 35.1 us
    pallas_call x1, Pallas kernels: 35.9 us -> 35.1 us  [on_device(): pl.pallas_call(functools.partial(kernel, n_space, n_tm), out_shape=(jax.S...]
where the time goes in v3:
time: 38.7 us; the launch traced here: 38.5 us
  Pallas kernels  35.1 us (91%)
  between operations  1.81 us (5%)
  local copies, waits for them, and re-layouts  1.68 us (4%)
    pallas_call x1, Pallas kernels, on_device(): pl.pallas_call(functools.partial(kernel, n_space, n_tm), out_shape=(jax.S...  35.1 us
    unnamed x3, local copies, waits for them, and re-layouts  1.68 us

profile of v3, /device:TPU:24, one launch (start us, length us, event | category | flops | bytes accessed | tf_op | source)
XLA Modules:
  0.0 38.5 jit_solution(4567120031285300178)
XLA Ops:
  0.6 35.1 %shard_map.59 = (f32[1,4,4,4,8,128]{5,4,3,2,1,0:T(8,128)}, f32[1,128]{1,0:T(1,128)}) custom-call(f32[1,4,4,4,8,128]{5,4,3,2,1,0:T(8,128)} %o_hbm.1, f32[4,8,128]{2,1,0:T(8,128)} %fac_hbm.1, f32[8,128]{1,0:T(8,128)} %bw_hbm.1, s32[8,128]{1,0:T(8,128)} %bf_hbm.1), custom_call_target="tpu_custom_call" | custom-call | tf_op jit(solution)/shard_map/pallas_call | solution.py:659
  35.7 0.0 copy-start
  35.7 1.7 %copy.8 = f32[1,4,4,4,8,128]{5,4,3,2,1,0:T(8,128)} copy(f32[1,4,4,4,8,128]{5,4,3,2,1,0:T(8,128)} %get-tuple-element.8) | data formatting | bytes 524288
  37.4 0.0 copy-done
Async XLA Ops:
  35.7 1.7 %copy-start = (f32[1,128]{1,0:T(1,128)S(1)}, f32[1,128]{1,0:T(1,128)}, u32[]{:S(2)}) copy-start(f32[1,128]{1,0:T(1,128)} %get-tuple-element.5) | copy-start | bytes 1540

commit v4 on v3

--- a/solution.py
+++ b/solution.py
@@ -382,8 +382,11 @@
                         value = value + keep * dst[v, t, j]
                     dst[v, t, j] = value
 
-        for t in range(4):
+        def across_step(t, _):
             across(t)
+            return 0
+
+        lax.fori_loop(0, 4, across_step, 0)
         for t in (1, 2):
             upward(t)
 

time: 38.7 us -> 39.1 us (1.010)
  no operation moved by 1% of the time
where the time goes in v4:
time: 39.1 us; the launch traced here: 38.9 us
  Pallas kernels  35.4 us (91%)
  between operations  1.81 us (5%)
  local copies, waits for them, and re-layouts  1.68 us (4%)
    pallas_call x1, Pallas kernels, on_device(): pl.pallas_call(functools.partial(kernel, n_space, n_tm), out_shape=(jax.S...  35.4 us
    unnamed x3, local copies, waits for them, and re-layouts  1.68 us

profile of v4, /device:TPU:24, one launch (start us, length us, event | category | flops | bytes accessed | tf_op | source)
XLA Modules:
  0.0 38.9 jit_solution(3623823104299767979)
XLA Ops:
  0.6 35.4 %shard_map.59 = (f32[1,4,4,4,8,128]{5,4,3,2,1,0:T(8,128)}, f32[1,128]{1,0:T(1,128)}) custom-call(f32[1,4,4,4,8,128]{5,4,3,2,1,0:T(8,128)} %o_hbm.1, f32[4,8,128]{2,1,0:T(8,128)} %fac_hbm.1, f32[8,128]{1,0:T(8,128)} %bw_hbm.1, s32[8,128]{1,0:T(8,128)} %bf_hbm.1), custom_call_target="tpu_custom_call" | custom-call | tf_op jit(solution)/shard_map/pallas_call | solution.py:662
  36.0 0.0 copy-start
  36.1 1.7 %copy.8 = f32[1,4,4,4,8,128]{5,4,3,2,1,0:T(8,128)} copy(f32[1,4,4,4,8,128]{5,4,3,2,1,0:T(8,128)} %get-tuple-element.8) | data formatting | bytes 524288
  37.7 0.0 copy-done
Async XLA Ops:
  36.0 1.7 %copy-start = (f32[1,128]{1,0:T(1,128)S(1)}, f32[1,128]{1,0:T(1,128)}, u32[]{:S(2)}) copy-start(f32[1,128]{1,0:T(1,128)} %get-tuple-element.5) | copy-start | bytes 1540
